TPU v7x, 128 devices: a whole 4x4x4 slice. The times are simulated.
128 devices in a mesh: dp: 16 (over y_hi, x, core), space: 8 (over z, y_lo).
Axes of the slice: x: 4, y: 4 (y_hi: 2, y_lo: 2; y = y_hi * 2 + y_lo), z: 4, core: 2. Of those that a mesh axis runs over, the one named last changes fastest.
Arguments:
- volume: bfloat16 [16, 32, 32, 128], P('dp', 'space'), may hold values from -6 to 6
- first_kernel: bfloat16 [3, 3, 3, 4, 64], replicated, may hold values from -0.625 to 0.625
- mid_kernel: bfloat16 [3, 3, 3, 64, 128], replicated, may hold values from -0.15625 to 0.15625
- deep_kernel: bfloat16 [3, 3, 3, 128, 256], replicated, may hold values from -0.109375 to 0.109375
- deep_cotangent: bfloat16 [16, 16, 16, 16, 256], P('dp', 'space'), may hold values from -6 to 6
Outputs:
- deep_output: bfloat16 [16, 16, 16, 16, 256], P('dp', 'space')
- deep_kernel_grad: float32 [3, 3, 3, 128, 256], P(None, None, None, 'space')
- mid_kernel_grad: float32 [3, 3, 3, 64, 128], replicated
All inputs are finite; a program needn't handle non-finite values.
Results may differ from a plain program's by a relative error of at most 0.024.
Values may be sent and summed in bfloat16 or wider, within the bound.
A program may use at most 128 MiB of HBM per device.

v0:
```python
import math
import jax
import jax.numpy as jnp
from jax import lax
from jax.sharding import PartitionSpec as P

SLOPE = 0.3


def padded_2(block, sides, width):
    for axis, dim in sides:
        count = lax.axis_size(axis)
        forward = [(i, i + 1) for i in range(count - 1)]
        backward = [(target, source) for source, target in forward]
        low = lax.ppermute(
            lax.slice_in_dim(block, block.shape[dim] - width, None, axis=dim), axis, forward
        )
        high = lax.ppermute(lax.slice_in_dim(block, 0, width, axis=dim), axis, backward)
        block = jnp.concatenate([low, block, high], axis=dim)
    return block


def activate(value):
    return SLOPE * value + (1.0 - SLOPE) * value * jax.nn.sigmoid(value)


def activate_slope(value):
    sig = jax.nn.sigmoid(value)
    return SLOPE + (1.0 - SLOPE) * (sig + value * sig * (1.0 - sig))


def conv_depth(padded, kernel):
    return lax.conv_general_dilated(
        padded[None],
        kernel,
        (1, 1, 1),
        [(0, 0), (1, 1), (1, 1)],
        dimension_numbers=("NDHWC", "DHWIO", "NDHWC"),
        preferred_element_type=jnp.float32,
    )[0]


def pool_cells(values):
    dd, hh, ww, cc = values.shape
    return values.reshape(dd // 2, 2, hh // 2, 2, ww // 2, 2, cc).mean(axis=(1, 3, 5))


def expand(values):
    return jnp.repeat(jnp.repeat(jnp.repeat(values, 2, 0), 2, 1), 2, 2)


def kernel_grad(padded, cotangent):
    dd, hh, ww, _ = cotangent.shape
    tap_list = []
    for depth_off in range(3):
        for row_off in range(3):
            for col_off in range(3):
                window = padded[
                    depth_off : depth_off + dd, row_off : row_off + hh, col_off : col_off + ww
                ]
                tap_list.append(
                    jnp.einsum(
                        "dhwi,dhwo->io", window, cotangent, preferred_element_type=jnp.float32
                    )
                )
    return jnp.stack(tap_list).reshape(3, 3, 3, padded.shape[-1], cotangent.shape[-1])


def pad_sides(values):
    return jnp.pad(values, ((0, 0), (1, 1), (1, 1), (0, 0)))


def pad_depth(values):
    return jnp.pad(values, ((1, 1), (0, 0), (0, 0), (0, 0)))


def pad_cells(values):
    return jnp.pad(values, ((1, 1), (1, 1), (1, 1), (0, 0)))


def on_device(volume, first_kernel, mid_kernel, deep_kernel, deep_cotangent):
    slab_depth = volume.shape[1]
    side_cells = volume.shape[2]
    in_channels = volume.shape[3] // side_cells
    space_count = lax.axis_size("space")
    space_index = lax.axis_index("space")
    input_field = volume[0].reshape(slab_depth, side_cells, side_cells, in_channels)
    padded = padded_2(input_field, (("space", 0),), 1)
    own_hidden = activate(conv_depth(padded, first_kernel)).astype(jnp.bfloat16)
    hidden = padded_2(own_hidden, (("space", 0),), 1)
    pre_mid = conv_depth(hidden, mid_kernel)
    pooled = pool_cells(activate(pre_mid)).astype(jnp.bfloat16)
    cotangent = deep_cotangent[0].astype(jnp.float32)
    columns = lax.all_to_all(pooled, "space", split_axis=3, concat_axis=0, tiled=True)
    chan_width = columns.shape[3]
    chan_start = space_index * chan_width
    kernel_part = lax.dynamic_slice_in_dim(deep_kernel, chan_start, chan_width, 3)
    partial_value = conv_depth(pad_depth(columns), kernel_part)
    pre_deep = lax.psum_scatter(partial_value, "space", scatter_dimension=0, tiled=True)
    grad_pre = (cotangent * activate_slope(pre_deep)).astype(jnp.bfloat16)
    all_cotangent = lax.all_gather(grad_pre, "space", axis=0, tiled=True)
    deep_grad = kernel_grad(pad_cells(columns), all_cotangent)
    flipped_part = jnp.swapaxes(kernel_part[::-1, ::-1, ::-1], 3, 4)
    back_grad = conv_depth(pad_depth(all_cotangent), flipped_part).astype(jnp.bfloat16)
    pooled_grad = lax.all_to_all(back_grad, "space", split_axis=0, concat_axis=3, tiled=True)
    deep_grad = lax.psum(deep_grad.astype(jnp.bfloat16), "dp").astype(jnp.float32)
    grad_mid = (expand(pooled_grad.astype(jnp.float32)) * 0.125 * activate_slope(pre_mid)).astype(
        jnp.bfloat16
    )
    mid_grad = lax.psum(kernel_grad(pad_sides(hidden), grad_mid), ("dp", "space"))
    device_total = lax.axis_size("dp") * space_count
    cell_count = slab_depth * side_cells * side_cells
    deep_scale = math.sqrt(device_total * cell_count // 8)
    mid_scale = math.sqrt(device_total * cell_count)
    deep_output = activate(pre_deep).astype(jnp.bfloat16)[None]
    return (deep_output, deep_grad / deep_scale, mid_grad / mid_scale)


def solution(mesh):
    in_specs = (P("dp", "space", None, None), P(), P(), P(), P("dp", "space", None, None, None))
    out_specs = (P("dp", "space", None, None, None), P(None, None, None, "space", None), P())
    return jax.shard_map(
        on_device, mesh=mesh, in_specs=in_specs, out_specs=out_specs, check_vma=False
    )
```

profile of v0, /device:TPU:1, one launch (start us, length us, event | category | flops | bytes accessed | tf_op | source)
XLA Modules:
  0.0 628.2 jit_solution(16983838333227108347)
XLA Ops:
  8.2 4.0 collective-permute-start
  13.6 3.4 collective-permute-done.1
  18.2 7.4 %add_convert_fusion = (bf16[4,32,8,5,64]{4,2,3,1,0:T(8,128)(2,1)}, f32[4,32,8,5,64]{4,2,3,1,0:T(8,128)S(1)}, f32[4,32,8,5,64]{4,2,3,1,0:T(8,128)S(1)}, f32[4,32,8,5,64]{4,2,3,1,0:T(8,128)S(1)}) fusion(pred[8,5]{0,1:T(8,128)(4,1)S(1)} %copy-done.21, bf16[3,3,3,4,64]{4,3,2,1,0:T(4,128)(2,1)S(1)} %copy-done.20, bf16[6,32,1,7,2,4]{3,5,4,1,0,2:T(4,128)(2,1)S(1)} %slice.257, ...), kind=kOutput, calls=%fused_computation.31 | convolution fusion | flops 72511488 | bytes 4684328 | tf_op jit(solution)/shard_map/conv_general_dilated | solution.py:33
  27.5 4.8 fusion.30
  32.4 4.3 collective-permute-start.2
  40.0 7.1 %collective-permute-done.3 = bf16[1,32,32,64]{3,2,1,0:T(8,128)(2,1)S(1)} collective-permute-done((bf16[1,32,32,64]{3,2,1,0:T(8,128)(2,1)S(1)}, bf16[1,32,32,64]{3,2,1,0:T(8,128)(2,1)S(1)}, u32[]{:S(2)}, u32[]{:S(2)}) %collective-permute-start.3) | collective-permute-done | bytes 131104 | tf_op jit(solution)/shard_map/ppermute | solution.py:18
  50.6 6.6 %broadcast_multiply_fusion.1 = (f32[4,32,8,5,128]{4,2,3,1,0:T(8,128)S(1)}, f32[4,32,8,5,128]{4,2,3,1,0:T(8,128)S(1)}, f32[4,32,8,5,128]{4,2,3,1,0:T(8,128)S(1)}, f32[4,32,8,5,128]{4,2,3,1,0:T(8,128)}) fusion(bf16[3,3,3,64,128]{4,3,2,1,0:T(8,128)(2,1)S(1)} %copy-done.19, bf16[6,32,1,7,2,64]{5,3,4,1,0,2:T(8,128)(2,1)S(1)} %slice.263, ...), kind=kOutput, calls=%fused_computation.97 | convolution fusion | flops 2225799168 | bytes 12255272 | tf_op jit(solution)/shard_map/conv_general_dilated | solution.py:33
  60.7 2.9 reduce_sum.9
  67.0 5.2 all-to-all-start
  72.3 5.5 all-to-all-done
  82.5 4.0 copy.321
  86.4 2.8 pad.24.clone
  89.3 5.7 copy.215
  96.8 4.5 broadcast_select_fusion
  106.2 93.6 %reduce-scatter.2.cloned.1.call-done = f32[2,16,16,256]{3,1,2,0:T(8,128)} async-done(((f32[16,16,16,256]{3,1,2,0:T(8,128)}), f32[2,16,16,256]{3,1,2,0:T(8,128)}) %reduce-scatter.2.cloned.1.call-update) | async-done | bytes 524304 | tf_op jit(solution)/shard_map/reduce_scatter | solution.py:99
  208.3 46.0 %all-gather.2.cloned.1.call-done = bf16[16,16,16,256]{3,2,1,0:T(8,128)(2,1)} async-done(((bf16[2,16,16,256]{3,2,1,0:T(8,128)(2,1)}), bf16[16,16,16,256]{3,2,1,0:T(8,128)(2,1)}) %all-gather.2.cloned.1.call-update) | async-done | bytes 2097168 | tf_op jit(solution)/shard_map/all_gather | solution.py:101
  259.6 22.7 %select_convert_fusion = bf16[16,16,8,3,16]{4,2,3,1,0:T(8,128)(2,1)S(1)} fusion(pred[8,3]{0,1:T(4,128)(4,1)S(1)} %copy-done.22, bf16[18,16,1,7,2,256]{5,3,4,1,0,2:T(8,128)(2,1)S(1)} %slice.269, bf16[18,16,1,8,3,256]{5,3,4,1,0,2:T(8,128)(2,1)S(1)} %copy.221, bf16[3,3,3,128,256]{4,3,2,1,0:T(8,128)(2,1)S(1)} %copy-done, s32[]{:T(128)S(6)} %select_n.3), kind=kOutput, calls=%fused_computation.13 | convolution fusion | flops 1320222720 | bytes 6316548 | tf_op jit(solution)/shard_map/conv_general_dilated | solution.py:33
  283.9 3.1 reshape.225
  287.0 3.4 all-to-all-start.1
  290.6 3.0 fusion.179
  293.5 2.9 fusion.177
  332.1 2.6 copy.314
  365.0 101.8 %all-reduce.7.cloned.1.call-done = bf16[3,3,3,16,256]{4,3,2,1,0:T(8,128)(2,1)} async-done(((bf16[3,3,3,16,256]{4,3,2,1,0:T(8,128)(2,1)}), bf16[3,3,3,16,256]{4,3,2,1,0:T(8,128)(2,1)}) %all-reduce.7.cloned.1.call-update) | async-done | bytes 221200 | tf_op jit(solution)/shard_map/psum | solution.py:106
  468.6 150.7 %all-reduce.9.cloned.1.call-done = f32[3,3,3,64,128]{4,3,2,1,0:T(8,128)} async-done(((f32[3,3,3,64,128]{4,3,2,1,0:T(8,128)}), f32[3,3,3,64,128]{4,3,2,1,0:T(8,128)}) %all-reduce.9.cloned.1.call-update) | async-done | bytes 884752 | tf_op jit(solution)/shard_map/psum | solution.py:110
  (167 shorter events, 115.6 us)
Async XLA Ops:
  7.2 89.5 %copy-start = (bf16[3,3,3,128,256]{4,3,2,1,0:T(8,128)(2,1)S(1)}, bf16[3,3,3,128,256]{4,3,2,1,0:T(8,128)(2,1)}, u32[]{:S(2)}) copy-start(bf16[3,3,3,128,256]{4,3,2,1,0:T(8,128)(2,1)} %param.8) | copy-start | bytes 5308420
  7.2 11.0 %copy-start.21 = (pred[8,5]{0,1:T(8,128)(4,1)S(1)}, pred[8,5]{0,1:T(8,128)(4,1)}, u32[]{:S(2)}) copy-start(pred[8,5]{0,1:T(8,128)(4,1)} %constant.63) | copy-start | bytes 124
  7.2 11.0 %copy-start.20 = (bf16[3,3,3,4,64]{4,3,2,1,0:T(4,128)(2,1)S(1)}, bf16[3,3,3,4,64]{4,3,2,1,0:T(4,128)(2,1)}, u32[]{:S(2)}) copy-start(bf16[3,3,3,4,64]{4,3,2,1,0:T(4,128)(2,1)} %param.6) | copy-start | bytes 41476
  8.2 5.3 collective-permute-start
  12.3 4.7 collective-permute-start.1
  32.3 16.2 %copy-start.6 = (bf16[4,32,1,32,64]{4,3,1,2,0:T(8,128)(2,1)}, bf16[4,32,1,32,64]{4,3,1,2,0:T(8,128)(2,1)S(1)}, u32[]{:S(2)}) copy-start(bf16[4,32,1,32,64]{4,3,1,2,0:T(8,128)(2,1)S(1)} %fusion.30) | copy-start | bytes 1572868
  32.4 7.6 %collective-permute-start.2 = (bf16[1,32,32,64]{3,2,1,0:T(8,128)(2,1)S(1)}, bf16[1,32,32,64]{3,2,1,0:T(8,128)(2,1)S(1)}, u32[]{:S(2)}, u32[]{:S(2)}) collective-permute-start(bf16[1,32,32,64]{3,2,1,0:T(8,128)(2,1)S(1)} %get-tuple-element.18), channel_id=1, source_target_pairs={{0,1},{1,2},{2,3},{3,4},{4,5},{5,6},{6,7},{8,9},{9,10},{10,11},{11... | collective-permute-start | bytes 393224 | tf_op jit(solution)/shard_map/ppermute | solution.py:15
  36.7 10.3 %collective-permute-start.3 = (bf16[1,32,32,64]{3,2,1,0:T(8,128)(2,1)S(1)}, bf16[1,32,32,64]{3,2,1,0:T(8,128)(2,1)S(1)}, u32[]{:S(2)}, u32[]{:S(2)}) collective-permute-start(bf16[1,32,32,64]{3,2,1,0:T(8,128)(2,1)S(1)} %get-tuple-element.19), channel_id=1, source_target_pairs={{1,0},{2,1},{3,2},{4,3},{5,4},{6,5},{7,6},{9,8},{10,9},{11,10},{12... | collective-permute-start | bytes 393224 | tf_op jit(solution)/shard_map/ppermute | solution.py:18
  40.0 8.6 %copy-start.16 = (bf16[1,32,32,64]{3,2,1,0:T(8,128)(2,1)}, bf16[1,32,32,64]{3,2,1,0:T(8,128)(2,1)S(1)}, u32[]{:S(2)}) copy-start(bf16[1,32,32,64]{3,2,1,0:T(8,128)(2,1)S(1)} %collective-permute-done.2) | copy-start | bytes 393220
  47.0 1.5 copy-start.14
  67.0 10.8 %all-to-all-start = ((bf16[8,2,4096]{2,1,0:T(2,128)(2,1)}), bf16[8,2,4096]{2,1,0:T(2,128)(2,1)S(1)}, u32[]{:S(2)}, u32[]{:S(2)}) async-start(bf16[8,2,4096]{2,1,0:T(2,128)(2,1)} %reshape.223), calls=%async_computation | async-start | bytes 262144 | tf_op jit(solution)/shard_map/all_to_all | solution.py:94
  72.3 127.6 %reduce-scatter.2.cloned.1.call-start = ((), (), s32[]{:S(2)}) async-start(), calls=%async_computation.3 | async-start | bytes 4718592 | tf_op jit(solution)/shard_map/reduce_scatter | solution.py:99
  89.3 7.4 %copy-start.22 = (pred[8,3]{0,1:T(4,128)(4,1)S(1)}, pred[8,3]{0,1:T(4,128)(4,1)}, u32[]{:S(2)}) copy-start(pred[8,3]{0,1:T(4,128)(4,1)} %constant.62) | copy-start | bytes 76
  94.9 1.8 copy-start.8
  105.7 94.1 %copy-start.13 = (bf16[1,2,16,16,256]{4,3,2,1,0:T(8,128)(2,1)S(1)}, bf16[1,2,16,16,256]{4,3,2,1,0:T(8,128)(2,1)}, u32[]{:S(2)}) copy-start(bf16[1,2,16,16,256]{4,3,2,1,0:T(8,128)(2,1)} %param.9) | copy-start | bytes 786436
  105.8 148.5 %all-gather.2.cloned.1.call-start = ((), (), s32[]{:S(2)}) async-start(), calls=%async_computation.4 | async-start | bytes 2359296 | tf_op jit(solution)/shard_map/all_gather | solution.py:101
  202.0 2.8 copy-start.9
  287.0 44.2 %all-to-all-start.1 = ((bf16[8,2,4096]{2,1,0:T(2,128)(2,1)}), bf16[8,2,4096]{2,1,0:T(2,128)(2,1)S(1)}, u32[]{:S(2)}, u32[]{:S(2)}) async-start(bf16[8,2,4096]{2,1,0:T(2,128)(2,1)} %reshape.225), calls=%async_computation.2 | async-start | bytes 262144 | tf_op jit(solution)/shard_map/all_to_all | solution.py:105
  290.4 176.5 %all-reduce.7.cloned.1.call-start = ((), (), s32[]{:S(2)}) async-start(), calls=%async_computation.5 | async-start | bytes 442368 | tf_op jit(solution)/shard_map/psum | solution.py:106
  293.5 2.9 copy-start.2
  331.1 288.2 %all-reduce.9.cloned.1.call-start = ((), (), s32[]{:S(2)}) async-start(), calls=%async_computation.6 | async-start | bytes 1769472 | tf_op jit(solution)/shard_map/psum | solution.py:110
  337.2 1.6 copy-start.5
  340.6 1.8 copy-start.4
  362.6 258.9 %copy-start.1 = (bf16[3,3,3,128,256]{4,3,2,1,0:T(8,128)(2,1)S(1)}, bf16[3,3,3,128,256]{4,3,2,1,0:T(8,128)(2,1)}, u32[]{:S(2)}) copy-start(bf16[3,3,3,128,256]{4,3,2,1,0:T(8,128)(2,1)} %param.8) | copy-start | bytes 5308420
  (9 other events, 10.2 us)
Sparse Core Ops, SparseCore 0:
  105.9 93.9 reduce-scatter.1
  202.2 52.0 all-gather.1
  331.2 135.5 all-reduce.6
  472.8 146.4 all-reduce.8
where the time goes:
time: 638 us; the launch traced here: 628 us
  waiting for transfers between devices  410 us (64%)
  matrix products  99 us (16%)
  local copies, waits for them, and re-layouts  65.3 us (10%)
  starting transfers between devices  20.2 us (3%)
  other arithmetic  18.8 us (3%)
  between operations  14.7 us (2%)
    psum x1, waiting for transfers between devices, on_device(): lax.psum(kernel_grad(pad_sides(hidden), grad_mid), ('dp', 'space'))  151 us
    psum x1, waiting for transfers between devices, on_device(): lax.psum(deep_grad.astype(jnp.bfloat16), 'dp').astype(jnp.float32)  102 us
    reduce_scatter x1, waiting for transfers between devices, on_device(): lax.psum_scatter(partial_value, 'space', scatter_dimension=0, tiled=True)  93.6 us
    dot_general x54, matrix products, kernel_grad(): jnp.einsum('dhwi,dhwo->io', window, cotangent, preferred_element_type=jnp...  57.9 us
    all_gather x1, waiting for transfers between devices, on_device(): all_cotangent = lax.all_gather(grad_pre, 'space', axis=0, tiled=True)  46 us
    conv_general_dilated x4, matrix products, conv_depth(): lax.conv_general_dilated(padded[None], kernel, (1, 1, 1), [(0, 0), (1, 1)...  41.1 us
    unnamed x55, local copies, waits for them, and re-layouts  22.3 us
    conv_general_dilated x11, local copies, waits for them, and re-layouts, conv_depth(): lax.conv_general_dilated(padded[None], kernel, (1, 1, 1), [(0, 0), (1, 1)...  15.4 us
  transfers between devices with their start and end apart: 10, of which 8 were waited for; matrix products, arithmetic and copies ran while one was open for 12% of the time, Pallas kernels for 0%

commit v1 on v0

--- a/solution.py
+++ b/solution.py
@@ -107,7 +107,9 @@
     grad_mid = (expand(pooled_grad.astype(jnp.float32)) * 0.125 * activate_slope(pre_mid)).astype(
         jnp.bfloat16
     )
-    mid_grad = lax.psum(kernel_grad(pad_sides(hidden), grad_mid), ("dp", "space"))
+    mid_grad = kernel_grad(pad_sides(hidden), grad_mid)
+    for dev_i in ("dp", "space"):
+        mid_grad = lax.psum(mid_grad, dev_i)
     device_total = lax.axis_size("dp") * space_count
     cell_count = slab_depth * side_cells * side_cells
     deep_scale = math.sqrt(device_total * cell_count // 8)

time: 638 us -> 739 us (1.16)
  waiting for transfers between devices: 410 us -> 503 us
    psum x1 -> x2, waiting for transfers between devices: 151 us -> 208 us  [on_device(): mid_grad = lax.psum(mid_grad, dev_i)]
    psum x1, waiting for transfers between devices: 102 us -> 137 us  [on_device(): lax.psum(deep_grad.astype(jnp.bfloat16), 'dp').astype(jnp.float32)]
    unnamed x55 -> x57, local copies, waits for them, and re-layouts: 22.3 us -> 22.3 us
  transfers between devices with their start and end apart: 10 -> 11, of which waited for: 8 -> 9; matrix products, arithmetic and copies ran while one was open for 12% -> 7% of each run, Pallas kernels for 0% -> 0%
where the time goes in v1:
time: 739 us; the launch traced here: 725 us
  waiting for transfers between devices  503 us (68%)
  matrix products  103 us (14%)
  local copies, waits for them, and re-layouts  65 us (9%)
  starting transfers between devices  20.3 us (3%)
  other arithmetic  18.7 us (3%)
  between operations  15 us (2%)
    psum x2, waiting for transfers between devices, on_device(): mid_grad = lax.psum(mid_grad, dev_i)  208 us
    psum x1, waiting for transfers between devices, on_device(): lax.psum(deep_grad.astype(jnp.bfloat16), 'dp').astype(jnp.float32)  137 us
    reduce_scatter x1, waiting for transfers between devices, on_device(): lax.psum_scatter(partial_value, 'space', scatter_dimension=0, tiled=True)  93.8 us
    dot_general x54, matrix products, kernel_grad(): jnp.einsum('dhwi,dhwo->io', window, cotangent, preferred_element_type=jnp...  61.2 us
    all_gather x1, waiting for transfers between devices, on_device(): all_cotangent = lax.all_gather(grad_pre, 'space', axis=0, tiled=True)  46 us
    conv_general_dilated x4, matrix products, conv_depth(): lax.conv_general_dilated(padded[None], kernel, (1, 1, 1), [(0, 0), (1, 1)...  41.6 us
    unnamed x57, local copies, waits for them, and re-layouts  22.3 us
    conv_general_dilated x11, local copies, waits for them, and re-layouts, conv_depth(): lax.conv_general_dilated(padded[None], kernel, (1, 1, 1), [(0, 0), (1, 1)...  15.4 us
  transfers between devices with their start and end apart: 11, of which 9 were waited for; matrix products, arithmetic and copies ran while one was open for 7% of the time, Pallas kernels for 0%

profile of v1, /device:TPU:1, one launch (start us, length us, event | category | flops | bytes accessed | tf_op | source)
XLA Modules:
  0.0 725.3 jit_solution(10784802462196196043)
XLA Ops:
  8.2 4.0 collective-permute-start
  13.6 3.4 collective-permute-done.1
  18.2 7.4 %add_convert_fusion = (bf16[4,32,8,5,64]{4,2,3,1,0:T(8,128)(2,1)}, f32[4,32,8,5,64]{4,2,3,1,0:T(8,128)S(1)}, f32[4,32,8,5,64]{4,2,3,1,0:T(8,128)S(1)}, f32[4,32,8,5,64]{4,2,3,1,0:T(8,128)S(1)}) fusion(pred[8,5]{0,1:T(8,128)(4,1)S(1)} %copy-done.22, bf16[3,3,3,4,64]{4,3,2,1,0:T(4,128)(2,1)S(1)} %copy-done.21, bf16[6,32,1,7,2,4]{3,5,4,1,0,2:T(4,128)(2,1)S(1)} %slice.257, ...), kind=kOutput, calls=%fused_computation.31 | convolution fusion | flops 72511488 | bytes 4684328 | tf_op jit(solution)/shard_map/conv_general_dilated | solution.py:33
  27.5 4.7 fusion.30
  32.3 4.3 collective-permute-start.2
  39.8 7.1 collective-permute-done.3
  50.5 6.6 broadcast_multiply_fusion.1
  66.9 5.2 all-to-all-start
  72.2 5.5 all-to-all-done
  82.4 4.0 copy.321
  89.1 5.7 copy.215
  96.6 4.5 broadcast_select_fusion
  105.9 93.8 %reduce-scatter.2.cloned.1.call-done = f32[2,16,16,256]{3,1,2,0:T(8,128)} async-done(((f32[16,16,16,256]{3,1,2,0:T(8,128)}), f32[2,16,16,256]{3,1,2,0:T(8,128)}) %reduce-scatter.2.cloned.1.call-update) | async-done | bytes 524304 | tf_op jit(solution)/shard_map/reduce_scatter | solution.py:99
  208.2 46.0 %all-gather.2.cloned.1.call-done = bf16[16,16,16,256]{3,2,1,0:T(8,128)(2,1)} async-done(((bf16[2,16,16,256]{3,2,1,0:T(8,128)(2,1)}), bf16[16,16,16,256]{3,2,1,0:T(8,128)(2,1)}) %all-gather.2.cloned.1.call-update) | async-done | bytes 2097168 | tf_op jit(solution)/shard_map/all_gather | solution.py:101
  259.5 23.2 %select_convert_fusion = bf16[16,16,8,3,16]{4,2,3,1,0:T(8,128)(2,1)S(1)} fusion(pred[8,3]{0,1:T(4,128)(4,1)S(1)} %copy-done.23, bf16[18,16,1,7,2,256]{5,3,4,1,0,2:T(8,128)(2,1)S(1)} %slice.269, bf16[18,16,1,8,3,256]{5,3,4,1,0,2:T(8,128)(2,1)S(1)} %copy.221, bf16[3,3,3,128,256]{4,3,2,1,0:T(8,128)(2,1)S(1)} %copy-done, s32[]{:T(128)S(6)} %select_n.3), kind=kOutput, calls=%fused_computation.13 | convolution fusion | flops 1320222720 | bytes 6316548 | tf_op jit(solution)/shard_map/conv_general_dilated | solution.py:33
  284.3 3.1 reshape.225
  287.4 3.4 all-to-all-start.1
  291.2 3.0 fusion.179
  294.2 2.9 fusion.177
  358.5 3.0 fusion.133
  361.5 3.2 fusion.131
  368.1 132.0 %all-reduce.10.cloned.1.call-done = f32[3,3,3,64,128]{4,3,2,1,0:T(8,128)} async-done(((f32[3,3,3,64,128]{4,3,2,1,0:T(8,128)}), f32[3,3,3,64,128]{4,3,2,1,0:T(8,128)}) %all-reduce.10.cloned.1.call-update) | async-done | bytes 884752 | tf_op jit(solution)/shard_map/psum | solution.py:112
  500.9 137.5 %all-reduce.8.cloned.1.call-done = bf16[3,3,3,16,256]{4,3,2,1,0:T(8,128)(2,1)} async-done(((bf16[3,3,3,16,256]{4,3,2,1,0:T(8,128)(2,1)}), bf16[3,3,3,16,256]{4,3,2,1,0:T(8,128)(2,1)}) %all-reduce.8.cloned.1.call-update) | async-done | bytes 221200 | tf_op jit(solution)/shard_map/psum | solution.py:106
  640.1 76.0 %all-reduce.12.cloned.1.call-done = f32[3,3,3,64,128]{4,3,2,1,0:T(8,128)} async-done(((f32[3,3,3,64,128]{4,3,2,1,0:T(8,128)}), f32[3,3,3,64,128]{4,3,2,1,0:T(8,128)}) %all-reduce.12.cloned.1.call-update) | async-done | bytes 884752 | tf_op jit(solution)/shard_map/psum | solution.py:112
  (172 shorter events, 121.0 us)
Async XLA Ops:
  7.2 89.4 %copy-start = (bf16[3,3,3,128,256]{4,3,2,1,0:T(8,128)(2,1)S(1)}, bf16[3,3,3,128,256]{4,3,2,1,0:T(8,128)(2,1)}, u32[]{:S(2)}) copy-start(bf16[3,3,3,128,256]{4,3,2,1,0:T(8,128)(2,1)} %param.8) | copy-start | bytes 5308420
  7.2 11.0 %copy-start.22 = (pred[8,5]{0,1:T(8,128)(4,1)S(1)}, pred[8,5]{0,1:T(8,128)(4,1)}, u32[]{:S(2)}) copy-start(pred[8,5]{0,1:T(8,128)(4,1)} %constant.63) | copy-start | bytes 124
  7.2 11.0 %copy-start.21 = (bf16[3,3,3,4,64]{4,3,2,1,0:T(4,128)(2,1)S(1)}, bf16[3,3,3,4,64]{4,3,2,1,0:T(4,128)(2,1)}, u32[]{:S(2)}) copy-start(bf16[3,3,3,4,64]{4,3,2,1,0:T(4,128)(2,1)} %param.6) | copy-start | bytes 41476
  8.2 5.3 collective-permute-start
  12.3 4.7 collective-permute-start.1
  32.2 16.2 %copy-start.7 = (bf16[4,32,1,32,64]{4,3,1,2,0:T(8,128)(2,1)}, bf16[4,32,1,32,64]{4,3,1,2,0:T(8,128)(2,1)S(1)}, u32[]{:S(2)}) copy-start(bf16[4,32,1,32,64]{4,3,1,2,0:T(8,128)(2,1)S(1)} %fusion.30) | copy-start | bytes 1572868
  32.3 7.6 %collective-permute-start.2 = (bf16[1,32,32,64]{3,2,1,0:T(8,128)(2,1)S(1)}, bf16[1,32,32,64]{3,2,1,0:T(8,128)(2,1)S(1)}, u32[]{:S(2)}, u32[]{:S(2)}) collective-permute-start(bf16[1,32,32,64]{3,2,1,0:T(8,128)(2,1)S(1)} %get-tuple-element.18), channel_id=1, source_target_pairs={{0,1},{1,2},{2,3},{3,4},{4,5},{5,6},{6,7},{8,9},{9,10},{10,11},{11... | collective-permute-start | bytes 393224 | tf_op jit(solution)/shard_map/ppermute | solution.py:15
  36.6 10.3 %collective-permute-start.3 = (bf16[1,32,32,64]{3,2,1,0:T(8,128)(2,1)S(1)}, bf16[1,32,32,64]{3,2,1,0:T(8,128)(2,1)S(1)}, u32[]{:S(2)}, u32[]{:S(2)}) collective-permute-start(bf16[1,32,32,64]{3,2,1,0:T(8,128)(2,1)S(1)} %get-tuple-element.19), channel_id=1, source_target_pairs={{1,0},{2,1},{3,2},{4,3},{5,4},{6,5},{7,6},{9,8},{10,9},{11,10},{12... | collective-permute-start | bytes 393224 | tf_op jit(solution)/shard_map/ppermute | solution.py:18
  39.8 8.6 %copy-start.17 = (bf16[1,32,32,64]{3,2,1,0:T(8,128)(2,1)}, bf16[1,32,32,64]{3,2,1,0:T(8,128)(2,1)S(1)}, u32[]{:S(2)}) copy-start(bf16[1,32,32,64]{3,2,1,0:T(8,128)(2,1)S(1)} %collective-permute-done.2) | copy-start | bytes 393220
  66.9 10.8 %all-to-all-start = ((bf16[8,2,4096]{2,1,0:T(2,128)(2,1)}), bf16[8,2,4096]{2,1,0:T(2,128)(2,1)S(1)}, u32[]{:S(2)}, u32[]{:S(2)}) async-start(bf16[8,2,4096]{2,1,0:T(2,128)(2,1)} %reshape.223), calls=%async_computation | async-start | bytes 262144 | tf_op jit(solution)/shard_map/all_to_all | solution.py:94
  72.1 127.6 %reduce-scatter.2.cloned.1.call-start = ((), (), s32[]{:S(2)}) async-start(), calls=%async_computation.3 | async-start | bytes 4718592 | tf_op jit(solution)/shard_map/reduce_scatter | solution.py:99
  89.1 7.4 %copy-start.23 = (pred[8,3]{0,1:T(4,128)(4,1)S(1)}, pred[8,3]{0,1:T(4,128)(4,1)}, u32[]{:S(2)}) copy-start(pred[8,3]{0,1:T(4,128)(4,1)} %constant.62) | copy-start | bytes 76
  94.8 1.8 copy-start.9
  105.6 94.1 %copy-start.14 = (bf16[1,2,16,16,256]{4,3,2,1,0:T(8,128)(2,1)S(1)}, bf16[1,2,16,16,256]{4,3,2,1,0:T(8,128)(2,1)}, u32[]{:S(2)}) copy-start(bf16[1,2,16,16,256]{4,3,2,1,0:T(8,128)(2,1)} %param.9) | copy-start | bytes 786436
  105.6 148.6 %all-gather.2.cloned.1.call-start = ((), (), s32[]{:S(2)}) async-start(), calls=%async_computation.4 | async-start | bytes 2359296 | tf_op jit(solution)/shard_map/all_gather | solution.py:101
  201.9 2.8 copy-start.10
  287.4 38.1 %all-to-all-start.1 = ((bf16[8,2,4096]{2,1,0:T(2,128)(2,1)}), bf16[8,2,4096]{2,1,0:T(2,128)(2,1)S(1)}, u32[]{:S(2)}, u32[]{:S(2)}) async-start(bf16[8,2,4096]{2,1,0:T(2,128)(2,1)} %reshape.225), calls=%async_computation.2 | async-start | bytes 262144 | tf_op jit(solution)/shard_map/all_to_all | solution.py:105
  290.7 209.3 %all-reduce.10.cloned.1.call-start = ((), (), s32[]{:S(2)}) async-start(), calls=%async_computation.6 | async-start | bytes 1769472 | tf_op jit(solution)/shard_map/psum | solution.py:112
  294.2 2.9 copy-start.2
  334.7 1.7 copy-start.5
  358.4 279.9 %all-reduce.8.cloned.1.call-start = ((), (), s32[]{:S(2)}) async-start(), calls=%async_computation.5 | async-start | bytes 442368 | tf_op jit(solution)/shard_map/psum | solution.py:106
  361.5 3.2 copy-start.3
  365.9 352.4 %copy-start.1 = (bf16[3,3,3,128,256]{4,3,2,1,0:T(8,128)(2,1)S(1)}, bf16[3,3,3,128,256]{4,3,2,1,0:T(8,128)(2,1)}, u32[]{:S(2)}) copy-start(bf16[3,3,3,128,256]{4,3,2,1,0:T(8,128)(2,1)} %param.8) | copy-start | bytes 5308420
  368.0 348.1 %all-reduce.12.cloned.1.call-start = ((), (), s32[]{:S(2)}) async-start(), calls=%async_computation.7 | async-start | bytes 1769472 | tf_op jit(solution)/shard_map/psum | solution.py:112
  (11 other events, 13.3 us)
Sparse Core Ops, SparseCore 0:
  105.7 93.9 reduce-scatter.1
  202.0 52.1 all-gather.1
  358.6 141.4 all-reduce.9
  503.1 135.1 all-reduce.7
  640.7 75.3 all-reduce.11
